TPU v7x, 256 devices: a whole 4x4x8 slice. The times are simulated.
256 devices in a mesh: segment: 4 (over x), tile: 64 (over z, y, core).
Axes of the slice: x: 4, y: 4, z: 8, core: 2. Of those that a mesh axis runs over, the one named last changes fastest.
Arguments:
- latent_clips: bfloat16 [4, 2, 256, 128, 128], P('segment', None, 'tile'), may hold values from -1.5 to 1.5
- augment_noise: bfloat16 [4, 4, 2, 256, 128, 128], P('segment', None, None, 'tile'), may hold values from -3.59375 to 3.59375
- section_weights: bfloat16 [4, 1152, 128], P('segment'), may hold values from -2 to 2
- frame_mixing: float32 [6, 128], replicated, may hold values from 0.1 to 0.9
- step_embed: float32 [6, 128], replicated, may hold values from -3 to 3
Outputs:
- sampled_clips: bfloat16 [4, 2, 256, 128, 128], P('segment', None, 'tile')
All inputs are finite; a program needn't handle non-finite values.
Results may differ from a plain program's by a relative error of at most 0.017.
Values may be sent and summed in bfloat16 or wider, within the bound.
A program may use at most 64 MiB of HBM per device.

v0:
```python
import functools

import jax
import jax.numpy as jnp
from jax import lax
from jax.experimental import pallas as pl
from jax.experimental.pallas import tpu as pltpu
from jax.sharding import PartitionSpec as P

MESH = pl.DeviceIdType.MESH
C = 128
COLS = 128
FRAMES = 2
STRIP = 4
HALO = 6
WIN = STRIP + 2 * HALO
NSEC = 4
NSTEP = 6
SECTION = (0, 0, 0, 1, 2, 3)
NEDGE = 3
NROWS = STRIP + 2 * NEDGE
SLICE = 9 * C // 8

norm_eps = 1e-06


def kernel(tiles, per_z, latent_ref, noise_ref, weight_ref, mix_ref, emb_ref, out_ref,
           aug, lat, mx, nz, wts,
           x_send, x_recv, wx_send, wx_recv, wz_send, wz_recv, wc_send, wc_recv,
           a_send, a_recv, n_send, n_recv, own_sem):
    me = lax.axis_index("segment")
    t = lax.axis_index("tile")
    core = lax.rem(t, 2)
    zq = lax.rem(t // per_z, 4)
    part = core * 4 + zq

    def tile_at(d):
        return lax.rem(t + d + tiles, tiles)

    def seg_at(d):
        return lax.rem(me + d, NSEC)

    def quad_at(d):
        return t + (lax.rem(zq + d, 4) - zq) * per_z

    partner = t + 1 - 2 * core

    own_noise = [
        pltpu.make_async_copy(
            noise_ref.at[0, me, :, pl.ds(2 * h, 2)],
            nz.at[me, :, pl.ds(NEDGE + 2 * h, 2)],
            x_recv.at[h, 0],
        )
        for h in range(2)
    ]
    own_weight = pltpu.make_async_copy(weight_ref.at[0], wts.at[me], own_sem)
    for c in own_noise:
        c.start()
    own_weight.start()

    barrier = pltpu.get_barrier_semaphore()
    others = [(seg_at(d), t) for d in (1, 2, 3)]
    others += [(me, quad_at(d)) for d in (1, 2, 3)]
    others += [(me, tile_at(d)) for d in (-2, -1, 1, 2)]
    for dev in others:
        pl.semaphore_signal(barrier, inc=1, device_id=dev, device_id_type=MESH)
    pl.semaphore_wait(barrier, len(others))

    rows_of = pl.ds(pl.multiple_of(part * SLICE, 16), SLICE)
    wx = {
        d: pltpu.make_async_remote_copy(
            src_ref=weight_ref.at[0, rows_of],
            dst_ref=wts.at[me, rows_of],
            send_sem=wx_send.at[d],
            recv_sem=wx_recv.at[d],
            device_id=(seg_at(d), t),
            device_id_type=MESH,
        )
        for d in (1, 2, 3)
    }
    nx = {
        (h, d): pltpu.make_async_remote_copy(
            src_ref=noise_ref.at[0, seg_at(d), :, pl.ds(2 * h, 2)],
            dst_ref=nz.at[me, :, pl.ds(NEDGE + 2 * h, 2)],
            send_sem=x_send.at[h, d],
            recv_sem=x_recv.at[h, d],
            device_id=(seg_at(d), t),
            device_id_type=MESH,
        )
        for d in (1, 2, 3)
        for h in range(2)
    }
    for d in (2, 1, 3):
        wx[d].start()
    even = lax.rem(me, 2) == 0
    for h in range(2):
        @pl.when(even)
        def _():
            nx[h, 2].start()
        nx[h, 1].start()
        nx[h, 3].start()

    wz = {}
    for j in (1, 2, 3):
        sec = lax.rem(me - j + NSEC, NSEC)
        for d in (1, 2, 3):
            wz[j, d] = pltpu.make_async_remote_copy(
                src_ref=wts.at[sec, rows_of],
                dst_ref=wts.at[sec, rows_of],
                send_sem=wz_send.at[j, d],
                recv_sem=wz_recv.at[j, d],
                device_id=(me, quad_at(d)),
                device_id_type=MESH,
            )
    for j in (1, 2, 3):
        wx[j].wait_recv()
        for d in (1, 2, 3):
            wz[j, d].start()

    def wait_noise(sec, h):
        piece = nz.at[sec, :, pl.ds(NEDGE + 2 * h, 2)]
        pltpu.make_async_copy(piece, piece, x_recv.at[h, lax.rem(me - sec + NSEC, NSEC)]).wait()

    def send_rows(i, row, count, to_row, d):
        return pltpu.make_async_remote_copy(
            src_ref=aug.at[pl.ds(HALO + row, count)],
            dst_ref=aug.at[pl.ds(to_row, count)],
            send_sem=a_send.at[i],
            recv_sem=a_recv.at[i],
            device_id=(me, tile_at(d)),
            device_id_type=MESH,
        )

    halo = [
        [send_rows(0, 0, 2, 10, -1), send_rows(1, 0, 2, 14, -2), send_rows(2, 0, 2, 2, 1)],
        [send_rows(3, 2, 2, 4, 1), send_rows(4, 2, 2, 0, 2), send_rows(5, 2, 2, 12, -1)],
    ]
    wc = {}
    for h in range(2):
        wait_noise(0, h)
        for row in (2 * h, 2 * h + 1):
            for f in range(FRAMES):
                aug[HALO + row, f] = (
                    latent_ref[0, f, row].astype(jnp.float32)
                    + 0.5 * nz[0, f, NEDGE + row].astype(jnp.float32)
                ).astype(jnp.bfloat16)
        for c in halo[h]:
            c.start()
        if h == 0:
            half = pl.ds(pl.multiple_of(core * 4 * SLICE, 16), 4 * SLICE)
            for j in (1, 2, 3):
                sec = lax.rem(me - j + NSEC, NSEC)
                for d in (1, 2, 3):
                    wz[j, d].wait_recv()
                wc[j] = pltpu.make_async_remote_copy(
                    src_ref=wts.at[sec, half],
                    dst_ref=wts.at[sec, half],
                    send_sem=wc_send.at[j],
                    recv_sem=wc_recv.at[j],
                    device_id=(me, partner),
                    device_id_type=MESH,
                )
                wc[j].start()

    @pl.when(jnp.logical_not(even))
    def _():
        for h in range(2):
            nx[h, 2].start()

    first = t * STRIP - HALO
    col = lax.broadcasted_iota(jnp.int32, (COLS, C), 0)
    left_edge = col == 0
    right_edge = col == COLS - 1

    def put_mixed(dst, row, k, pair):
        valid = jnp.logical_and(first + row >= 0, first + row < tiles * STRIP)
        mean = 0.5 * (pair[0] + pair[1])
        factor = mix_ref[k:k + 1, :]
        for f in range(FRAMES):
            mixed = pair[f] + factor * (mean - pair[f])
            mixed = jnp.where(valid, mixed, 0.0)
            mx[dst, 1, row, f] = mixed.astype(jnp.bfloat16)
            mx[dst, 0, row, f] = jnp.where(left_edge, 0.0, pltpu.roll(mixed, 1, 0)).astype(jnp.bfloat16)
            mx[dst, 2, row, f] = jnp.where(right_edge, 0.0, pltpu.roll(mixed, COLS - 1, 0)).astype(jnp.bfloat16)

    def mix_rows(lo, count):
        def body(i, _):
            row = lo + i
            put_mixed(0, row, 0, [aug[row, f].astype(jnp.float32) for f in range(FRAMES)])
            return 0
        lax.fori_loop(0, count, body, 0)

    mix_rows(HALO, STRIP)
    for i in (0, 2, 3, 5, 1, 4):
        halo[i // 3][i % 3].wait_recv()
    mix_rows(0, HALO)
    mix_rows(HALO + STRIP, HALO)

    own_weight.wait()
    for j in (1, 2, 3):
        wc[j].wait_recv()

    def step(k):
        sec = SECTION[k]
        src, dst = k % 2, (k + 1) % 2
        lat_in = aug if k == 0 else lat
        entering = k + 1 < NSTEP and SECTION[k + 1] != sec

        def body(p, _):
            base = k + 2 * p
            lhs = jnp.concatenate(
                [
                    mx[src, b, base + i].reshape(FRAMES * COLS, C)
                    for i in range(4)
                    for b in range(3)
                ],
                axis=1,
            )
            w = wts[sec]
            none = jnp.zeros((3 * C, C), jnp.bfloat16)
            rhs = jnp.concatenate(
                [jnp.concatenate([w, none], axis=0), jnp.concatenate([none, w], axis=0)], axis=1
            )
            acc = jnp.dot(lhs, rhs, preferred_element_type=jnp.float32)
            for j in range(2):
                row = base + 1 + j
                conv = acc[:, j * C:(j + 1) * C] + emb_ref[k:k + 1, :]
                power = jnp.mean(conv * conv, axis=-1, keepdims=True)
                half = conv * (0.5 * lax.rsqrt(power + norm_eps))
                silu = half + half * jnp.tanh(half)
                old = lat_in[row].reshape(FRAMES * COLS, C).astype(jnp.float32)
                new = (0.9 * old + 0.5 * silu).astype(jnp.bfloat16)
                if k == NSTEP - 1:
                    for f in range(FRAMES):
                        out_ref[0, f, row - HALO] = new[f * COLS:(f + 1) * COLS]
                    continue
                pair = [new[f * COLS:(f + 1) * COLS] for f in range(FRAMES)]
                if entering:
                    pair = [
                        (
                            v.astype(jnp.float32)
                            + 0.5 * nz[sec + 1, f, row - HALO + NEDGE].astype(jnp.float32)
                        ).astype(jnp.bfloat16)
                        for f, v in enumerate(pair)
                    ]
                for f in range(FRAMES):
                    lat[row, f] = pair[f]
                put_mixed(dst, row, k + 1, [v.astype(jnp.float32) for v in pair])
            return 0

        lax.fori_loop(0, (WIN - 2 * (k + 1)) // 2, body, 0)

    edge = {}

    def forward_noise(sec):
        count = NEDGE - (sec - 1)
        for h in range(2):
            wait_noise(sec, h)
        for i, (lo, to, d) in enumerate(
            ((NEDGE, NEDGE + STRIP, -1), (NEDGE + STRIP - count, NEDGE - count, 1))
        ):
            edge[sec, i] = pltpu.make_async_remote_copy(
                src_ref=nz.at[sec, :, pl.ds(lo, count)],
                dst_ref=nz.at[sec, :, pl.ds(to, count)],
                send_sem=n_send.at[sec - 1, i],
                recv_sem=n_recv.at[sec - 1, i],
                device_id=(me, tile_at(d)),
                device_id_type=MESH,
            )
            edge[sec, i].start()

    def wait_edge(sec):
        for i in range(2):
            edge[sec, i].wait_recv()

    step(0)
    forward_noise(1)
    step(1)
    forward_noise(2)
    forward_noise(3)
    wait_edge(1)
    step(2)
    wait_edge(2)
    step(3)
    wait_edge(3)
    step(4)
    step(5)

    for d in (1, 2, 3):
        wx[d].wait_send()
        wc[d].wait_send()
        for h in range(2):
            nx[h, d].wait_send()
        for e in (1, 2, 3):
            wz[d, e].wait_send()
        for i in range(2):
            edge[d, i].wait_send()
    for pieces in halo:
        for c in pieces:
            c.wait_send()


def build(mesh, per_z):
    tiles = mesh.shape["tile"]
    bf = jnp.bfloat16
    dma = pltpu.SemaphoreType.DMA

    def per_device(latent_clips, augment_noise, section_weights, frame_mixing, step_embed):
        vmem = pl.BlockSpec(memory_space=pltpu.VMEM)
        hbm = pl.BlockSpec(memory_space=pl.ANY)
        return pl.pallas_call(
            functools.partial(kernel, tiles, per_z),
            out_shape=jax.ShapeDtypeStruct(latent_clips.shape, bf),
            in_specs=[vmem, hbm, hbm, vmem, vmem],
            out_specs=vmem,
            scratch_shapes=[
                pltpu.VMEM((WIN, FRAMES, COLS, C), bf),
                pltpu.VMEM((WIN, FRAMES, COLS, C), bf),
                pltpu.VMEM((2, 3, WIN, FRAMES, COLS, C), bf),
                pltpu.VMEM((NSEC, FRAMES, NROWS, COLS, C), bf),
                pltpu.VMEM((NSEC, 9 * C, C), bf),
                dma((2, 4)), dma((2, 4)),
                dma((4,)), dma((4,)),
                dma((4, 4)), dma((4, 4)),
                dma((4,)), dma((4,)),
                dma((6,)), dma((6,)),
                dma((3, 2)), dma((3, 2)),
                dma,
            ],
            compiler_params=pltpu.CompilerParams(
                collective_id=0, has_side_effects=True, vmem_limit_bytes=48 << 20
            ),
        )(latent_clips, augment_noise, section_weights, frame_mixing, step_embed)

    return jax.shard_map(
        per_device,
        mesh=mesh,
        in_specs=(
            P("segment", None, "tile", None, None),
            P("segment", None, None, "tile", None, None),
            P("segment", None, None),
            P(),
            P(),
        ),
        out_specs=P("segment", None, "tile", None, None),
        check_vma=False,
    )


def solution(mesh):
    return build(mesh, 8)
```

profile of v0, /device:TPU:2, one launch (start us, length us, event | category | flops | bytes accessed | tf_op | source)
XLA Modules:
  0.0 53.1 jit_solution(14893287929108099840)
XLA Ops:
  0.0 0.0 copy-start
  0.0 1.2 %copy-done = bf16[1,4,2,4,128,128]{5,4,3,2,1,0:T(8,128)(2,1)S(1)} copy-done((bf16[1,4,2,4,128,128]{5,4,3,2,1,0:T(8,128)(2,1)S(1)}, bf16[1,4,2,4,128,128]{5,4,3,2,1,0:T(8,128)(2,1)}, u32[]{:S(2)}) %copy-start) | copy-done | bytes 1048600
  1.2 0.0 copy-start.1
  1.2 1.0 %copy-done.1 = bf16[1,1152,128]{2,1,0:T(8,128)(2,1)S(1)} copy-done((bf16[1,1152,128]{2,1,0:T(8,128)(2,1)S(1)}, bf16[1,1152,128]{2,1,0:T(8,128)(2,1)}, u32[]{:S(2)}) %copy-start.1) | copy-done | bytes 294936
  2.2 0.0 copy-start.2
  2.2 0.9 %copy-done.2 = bf16[1,2,4,128,128]{4,3,2,1,0:T(8,128)(2,1)S(1)} copy-done((bf16[1,2,4,128,128]{4,3,2,1,0:T(8,128)(2,1)S(1)}, bf16[1,2,4,128,128]{4,3,2,1,0:T(8,128)(2,1)}, u32[]{:S(2)}) %copy-start.2) | copy-done | bytes 262168
  3.1 0.0 copy-start.3
  3.1 0.7 %copy-done.3 = f32[6,128]{1,0:T(8,128)S(1)} copy-done((f32[6,128]{1,0:T(8,128)S(1)}, f32[6,128]{1,0:T(8,128)}, u32[]{:S(2)}) %copy-start.3) | copy-done | bytes 3096
  3.8 0.0 copy-start.4
  3.8 0.7 %copy-done.4 = f32[6,128]{1,0:T(8,128)S(1)} copy-done((f32[6,128]{1,0:T(8,128)S(1)}, f32[6,128]{1,0:T(8,128)}, u32[]{:S(2)}) %copy-start.4) | copy-done | bytes 3096
  4.5 47.9 %shard_map.55 = bf16[1,2,4,128,128]{4,3,2,1,0:T(8,128)(2,1)S(1)} custom-call(bf16[1,2,4,128,128]{4,3,2,1,0:T(8,128)(2,1)S(1)} %copy-done.2, bf16[1,4,2,4,128,128]{5,4,3,2,1,0:T(8,128)(2,1)S(1)} %copy-done, bf16[1,1152,128]{2,1,0:T(8,128)(2,1)S(1)} %copy-done.1, f32[6,128]{1,0:T(8,128)S(1)} %copy-done.3, f32[6,128]{1,0:T(8,128)S(1)} %copy-done.4), custom_call_target="tpu_custom_call" | custom-call | tf_op jit(solution)/shard_map/pallas_call | solution.py:311
  52.4 0.7 %copy.7 = bf16[1,2,4,128,128]{4,3,2,1,0:T(8,128)(2,1)} copy(bf16[1,2,4,128,128]{4,3,2,1,0:T(8,128)(2,1)S(1)} %shard_map.55) | data formatting | bytes 524288
Async XLA Ops:
  0.0 1.2 %copy-start = (bf16[1,4,2,4,128,128]{5,4,3,2,1,0:T(8,128)(2,1)S(1)}, bf16[1,4,2,4,128,128]{5,4,3,2,1,0:T(8,128)(2,1)}, u32[]{:S(2)}) copy-start(bf16[1,4,2,4,128,128]{5,4,3,2,1,0:T(8,128)(2,1)} %noise_ref.1) | copy-start | bytes 3145732
  1.2 1.0 %copy-start.1 = (bf16[1,1152,128]{2,1,0:T(8,128)(2,1)S(1)}, bf16[1,1152,128]{2,1,0:T(8,128)(2,1)}, u32[]{:S(2)}) copy-start(bf16[1,1152,128]{2,1,0:T(8,128)(2,1)} %weight_ref.1) | copy-start | bytes 884740
  2.2 0.9 %copy-start.2 = (bf16[1,2,4,128,128]{4,3,2,1,0:T(8,128)(2,1)S(1)}, bf16[1,2,4,128,128]{4,3,2,1,0:T(8,128)(2,1)}, u32[]{:S(2)}) copy-start(bf16[1,2,4,128,128]{4,3,2,1,0:T(8,128)(2,1)} %latent_ref.1) | copy-start | bytes 786436
  3.1 0.7 %copy-start.3 = (f32[6,128]{1,0:T(8,128)S(1)}, f32[6,128]{1,0:T(8,128)}, u32[]{:S(2)}) copy-start(f32[6,128]{1,0:T(8,128)} %mix_ref.1) | copy-start | bytes 9220
  3.8 0.7 %copy-start.4 = (f32[6,128]{1,0:T(8,128)S(1)}, f32[6,128]{1,0:T(8,128)}, u32[]{:S(2)}) copy-start(f32[6,128]{1,0:T(8,128)} %emb_ref.1) | copy-start | bytes 9220
where the time goes:
time: 53.3 us; the launch traced here: 53.1 us
  Pallas kernels  47.9 us (90%)
  local copies, waits for them, and re-layouts  5.21 us (10%)
    pallas_call x1, Pallas kernels, per_device(): pl.pallas_call(functools.partial(kernel, tiles, per_z), out_shape=jax.Sha...  47.9 us
    unnamed x11, local copies, waits for them, and re-layouts  5.21 us

commit v1 on v0

v1 whole, which is shorter than its diff:
```python
import functools

import jax
import jax.numpy as jnp
from jax import lax
from jax.experimental import pallas as pl
from jax.experimental.pallas import tpu as pltpu
from jax.sharding import PartitionSpec as P

MESH = pl.DeviceIdType.MESH
C = 128
COLS = 128
FRAMES = 2
STRIP = 4
HALO = 6
WIN = STRIP + 2 * HALO
NSEC = 4
NSTEP = 6
SECTION = (0, 0, 0, 1, 2, 3)
NEDGE = 3
NROWS = STRIP + 2 * NEDGE
SLICE = 9 * C // 8
GROUPS = {6: (3, 3), 5: (3, 2), 4: (4,), 3: (3,), 2: (2,)}
WIDEST = 4
ROW_ORDER = (0, 3, 1, 2)

norm_eps = 1e-06


def kernel(tiles, per_z, latent_hbm, noise_ref, weight_ref, mix_hbm, emb_hbm, out_ref,
           aug, lat, mxa, mxb, nz, wts, latent_ref, mix_ref, emb_ref, shift,
           f_send, f_recv, x_send, x_recv, wx_send, wx_recv, wz_send, wz_recv, wc_send, wc_recv,
           a_send, a_recv, n_send, n_recv, own_sem):
    me = lax.axis_index("segment")
    t = lax.axis_index("tile")
    core = lax.rem(t, 2)
    zq = lax.rem(t // per_z, 4)
    part = core * 4 + zq
    partner = t + 1 - 2 * core
    mx = (mxa, mxb)

    def tile_at(d):
        return lax.rem(t + d + tiles, tiles)

    def seg_at(d):
        return lax.rem(me + d, NSEC)

    def quad_at(d):
        return t + (lax.rem(zq + d, 4) - zq) * per_z

    def remote(src, dst, send, recv, seg, tile):
        return pltpu.make_async_remote_copy(
            src_ref=src,
            dst_ref=dst,
            send_sem=send,
            recv_sem=recv,
            device_id=(seg, tile),
            device_id_type=MESH,
        )

    def arrived(ref, sem):
        pltpu.make_async_copy(ref, ref, sem).wait()

    barrier = pltpu.get_barrier_semaphore()
    others = [(seg_at(d), t) for d in (1, 2, 3)]
    others += [(me, quad_at(d)) for d in (1, 2, 3)]
    others += [(me, tile_at(d)) for d in (-2, -1, 1, 2)]
    for dev in others:
        pl.semaphore_signal(barrier, inc=1, device_id=dev, device_id_type=MESH)

    def first_noise(row):
        return nz.at[0, :, pl.ds(NEDGE + row, 1)]

    def later_noise(sec):
        return nz.at[sec, :, pl.ds(NEDGE, STRIP)]

    own_weight = pltpu.make_async_copy(weight_ref.at[0], wts.at[me], own_sem.at[0])
    own_rest = [
        pltpu.make_async_copy(latent_hbm.at[0], latent_ref, own_sem.at[1]),
        pltpu.make_async_copy(mix_hbm, mix_ref, own_sem.at[2]),
        pltpu.make_async_copy(emb_hbm, emb_ref, own_sem.at[3]),
    ]
    for c in own_rest:
        c.start()

    @pl.when(me == 0)
    def _():
        for row in ROW_ORDER:
            pltpu.make_async_copy(
                noise_ref.at[0, me, :, pl.ds(row, 1)], first_noise(row), f_recv.at[row]
            ).start()

    @pl.when(me != 0)
    def _():
        pltpu.make_async_copy(noise_ref.at[0, me], later_noise(me), x_recv.at[me]).start()

    own_weight.start()
    for side in (0, COLS + 8):
        shift[:, pl.ds(side, 8)] = jnp.zeros((4 * WIDEST, 8, C), jnp.float32)
    pl.semaphore_wait(barrier, len(others))

    rows_of = pl.ds(pl.multiple_of(part * SLICE, 16), SLICE)
    half = pl.ds(pl.multiple_of(core * 4 * SLICE, 16), 4 * SLICE)

    def slice_to(d):
        return remote(weight_ref.at[0, rows_of], wts.at[me, rows_of],
                      wx_send.at[d], wx_recv.at[me], seg_at(d), t)

    def first_to(row, d):
        return remote(noise_ref.at[0, seg_at(d), :, pl.ds(row, 1)], first_noise(row),
                      f_send.at[row, d], f_recv.at[row], seg_at(d), t)

    def later_to(d):
        return remote(noise_ref.at[0, seg_at(d)], later_noise(me),
                      x_send.at[d], x_recv.at[me], seg_at(d), t)

    def gather(sec, d):
        return remote(wts.at[sec, rows_of], wts.at[sec, rows_of],
                      wz_send.at[sec, d], wz_recv.at[sec, d], me, quad_at(d))

    def share(sec):
        return remote(wts.at[sec, half], wts.at[sec, half],
                      wc_send.at[sec], wc_recv.at[sec], me, partner)

    for d in (2, 1, 3):
        slice_to(d).start()

    @pl.when(me == 0)
    def _():
        for row in ROW_ORDER:
            for d in (2, 1, 3):
                first_to(row, d).start()

    for sec, early in ((1, (3, 1)), (2, (2, 1, 3)), (3, (1, 3))):
        @pl.when(me == sec)
        def _(early=early):
            for d in early:
                later_to(d).start()

    def start_gather(sec):
        @pl.when(me != sec)
        def _():
            arrived(wts.at[sec, rows_of], wx_recv.at[sec])
            for d in (1, 2, 3):
                gather(sec, d).start()

    def start_share(sec):
        @pl.when(me != sec)
        def _():
            for d in (1, 2, 3):
                gather(sec, d).wait_recv()
            share(sec).start()

    def finish_share(sec):
        @pl.when(me != sec)
        def _():
            share(sec).wait_recv()

    start_gather(0)

    def row_copy(row, i):
        far = (14 + row, -2) if row < 2 else (row - 2, 2)
        to, d = ((10 + row, -1), (2 + row, 1), far)[i]
        return remote(aug.at[pl.ds(HALO + row, 1)], aug.at[pl.ds(to, 1)],
                      a_send.at[row, i], a_recv.at[row, i], me, tile_at(d))

    for c in own_rest:
        c.wait()
    for row in ROW_ORDER:
        arrived(first_noise(row), f_recv.at[row])
        for f in range(FRAMES):
            aug[HALO + row, f] = (
                latent_ref[f, row].astype(jnp.float32)
                + 0.5 * nz[0, f, NEDGE + row].astype(jnp.float32)
            ).astype(jnp.bfloat16)
        for i in range(3):
            row_copy(row, i).start()

    @pl.when(lax.rem(me, 2) == 1)
    def _():
        later_to(2).start()

    start_share(0)

    first = t * STRIP - HALO

    def put_mixed(dst, row, k, pair, slot):
        change = (0.5 * mix_ref[k:k + 1, :]) * (pair[1] - pair[0])
        for f, mixed in enumerate((pair[0] + change, pair[1] - change)):
            wide = shift.at[slot + f]
            wide[pl.ds(8, COLS)] = mixed
            mx[dst][1, row, f] = mixed.astype(jnp.bfloat16)
            mx[dst][0, row, f] = wide[pl.ds(7, COLS)].astype(jnp.bfloat16)
            mx[dst][2, row, f] = wide[pl.ds(9, COLS)].astype(jnp.bfloat16)

    def blank_outside(dst):
        zero = jnp.zeros((3, 1, FRAMES, COLS, C), jnp.bfloat16)

        def blank(row, _):
            mx[dst][:, pl.ds(row, 1)] = zero
            return 0

        @pl.when(first < 0)
        def _():
            lax.fori_loop(0, -first, blank, 0)

        @pl.when(first + WIN > tiles * STRIP)
        def _():
            lax.fori_loop(tiles * STRIP - first, WIN, blank, 0)

    def mix_rows(lo, count):
        def body(i, _):
            for j in range(2):
                row = lo + 2 * i + j
                put_mixed(0, row, 0, [aug[row, f].astype(jnp.float32) for f in range(FRAMES)], 2 * j)
            return 0
        lax.fori_loop(0, count // 2, body, 0)

    def step(k, bases=None):
        sec = SECTION[k]
        src, dst = k % 2, (k + 1) % 2
        lat_in = aug if k == 0 else lat
        entering = k + 1 < NSTEP and SECTION[k + 1] != sec

        def conv_of(base):
            lhs = jnp.concatenate(
                [
                    mx[src][b, base + i].reshape(FRAMES * COLS, C)
                    for i in range(4)
                    for b in range(3)
                ],
                axis=1,
            )
            w = wts[sec]
            none = jnp.zeros((3 * C, C), jnp.bfloat16)
            rhs = jnp.concatenate(
                [jnp.concatenate([w, none], axis=0), jnp.concatenate([none, w], axis=0)], axis=1
            )
            return jnp.dot(lhs, rhs, preferred_element_type=jnp.float32)

        def finish(base, acc, slot):
            for j in range(2):
                row = base + 1 + j
                conv = acc[:, j * C:(j + 1) * C] + emb_ref[k:k + 1, :]
                power = jnp.sum(conv * conv, axis=-1, keepdims=True)
                half = conv * lax.rsqrt(power * (4.0 / C) + 4.0 * norm_eps)
                old = lat_in[row].reshape(FRAMES * COLS, C).astype(jnp.float32)
                new = (0.9 * old + (0.5 * half) * (1.0 + jnp.tanh(half))).astype(jnp.bfloat16)
                if k == NSTEP - 1:
                    for f in range(FRAMES):
                        out_ref[0, f, row - HALO] = new[f * COLS:(f + 1) * COLS]
                    continue
                pair = [new[f * COLS:(f + 1) * COLS] for f in range(FRAMES)]
                if entering:
                    pair = [
                        (
                            v.astype(jnp.float32)
                            + 0.5 * nz[sec + 1, f, row - HALO + NEDGE].astype(jnp.float32)
                        ).astype(jnp.bfloat16)
                        for f, v in enumerate(pair)
                    ]
                for f in range(FRAMES):
                    lat[row, f] = pair[f]
                put_mixed(dst, row, k + 1, [v.astype(jnp.float32) for v in pair], slot + 2 * j)

        def several(bases):
            accs = [conv_of(base) for base in bases]
            for i, base in enumerate(bases):
                finish(base, accs[i], 4 * i)

        def run(lo, groups):
            times = len(groups) if len(set(groups)) == 1 else 1
            if times == 1:
                for take in groups:
                    several([lo + 2 * i for i in range(take)])
                    lo += 2 * take
                return
            take = groups[0]

            def body(p, _):
                several([lo + 2 * (p * take + i) for i in range(take)])
                return 0

            lax.fori_loop(0, times, body, 0)

        if bases is not None:
            several(bases)
        else:
            run(k, GROUPS[(WIN - 2 * (k + 1)) // 2])
        if k < NSTEP - 1 and bases is None:
            blank_outside(dst)

    edge = {}

    def forward_noise(sec):
        count = NEDGE - (sec - 1)
        arrived(later_noise(sec), x_recv.at[sec])
        for i, (lo, to, d) in enumerate(
            ((NEDGE, NEDGE + STRIP, -1), (NEDGE + STRIP - count, NEDGE - count, 1))
        ):
            edge[sec, i] = remote(
                nz.at[sec, :, pl.ds(lo, count)], nz.at[sec, :, pl.ds(to, count)],
                n_send.at[sec - 1, i], n_recv.at[sec - 1, i], me, tile_at(d),
            )
            edge[sec, i].start()

    def wait_edge(sec):
        for i in range(2):
            edge[sec, i].wait_recv()

    chip = HALO - STRIP * core
    mix_rows(HALO, STRIP)
    near = (HALO + STRIP) - 2 * STRIP * core
    for row in range(STRIP):
        arrived(aug.at[pl.ds(near + row, 1)], a_recv.at[row, core])
    mix_rows(near, STRIP)
    own_weight.wait()
    finish_share(0)
    step(0, [chip + 2 * i for i in range(3)])
    for sec in (1, 2, 3):
        start_gather(sec)
    over = (HALO - STRIP) + 2 * STRIP * core
    for row in range(STRIP):
        arrived(aug.at[pl.ds(over + row, 1)], a_recv.at[row, 1 - core])
    mix_rows(over, STRIP)
    for row in range(STRIP):
        row_copy(row, 2).wait_recv()
    mix_rows(0, 2)
    mix_rows(WIN - 2, 2)
    blank_outside(0)
    step(0, [lax.rem(chip + 6 + 2 * i, 14) for i in range(4)])
    blank_outside(1)
    forward_noise(1)
    step(1)
    for sec in (1, 2, 3):
        start_share(sec)
    forward_noise(2)
    forward_noise(3)
    wait_edge(1)
    step(2)
    finish_share(1)
    wait_edge(2)
    step(3)
    finish_share(2)
    wait_edge(3)
    step(4)
    finish_share(3)
    step(5)

    for d in (1, 2, 3):
        slice_to(d).wait_send()
        for i in range(2):
            edge[d, i].wait_send()

    @pl.when(me == 0)
    def _():
        for row in ROW_ORDER:
            for d in (1, 2, 3):
                first_to(row, d).wait_send()

    @pl.when(me != 0)
    def _():
        for d in (1, 2, 3):
            later_to(d).wait_send()

    for sec in range(NSEC):
        @pl.when(me != sec)
        def _(sec=sec):
            for d in (1, 2, 3):
                gather(sec, d).wait_send()
            share(sec).wait_send()

    for row in range(STRIP):
        for i in range(3):
            row_copy(row, i).wait_send()


def build(mesh, per_z):
    tiles = mesh.shape["tile"]
    bf = jnp.bfloat16
    dma = pltpu.SemaphoreType.DMA

    def per_device(latent_clips, augment_noise, section_weights, frame_mixing, step_embed):
        vmem = pl.BlockSpec(memory_space=pltpu.VMEM)
        hbm = pl.BlockSpec(memory_space=pltpu.HBM)
        return pl.pallas_call(
            functools.partial(kernel, tiles, per_z),
            out_shape=jax.ShapeDtypeStruct(latent_clips.shape, bf),
            in_specs=[hbm, hbm, hbm, hbm, hbm],
            out_specs=vmem,
            scratch_shapes=[
                pltpu.VMEM((WIN, FRAMES, COLS, C), bf),
                pltpu.VMEM((WIN, FRAMES, COLS, C), bf),
                pltpu.VMEM((3, WIN, FRAMES, COLS, C), bf),
                pltpu.VMEM((3, WIN, FRAMES, COLS, C), bf),
                pltpu.VMEM((NSEC, FRAMES, NROWS, COLS, C), bf),
                pltpu.VMEM((NSEC, 9 * C, C), bf),
                pltpu.VMEM((FRAMES, STRIP, COLS, C), bf),
                pltpu.VMEM((NSTEP, C), jnp.float32),
                pltpu.VMEM((NSTEP, C), jnp.float32),
                pltpu.VMEM((4 * WIDEST, COLS + 16, C), jnp.float32),
                dma((STRIP, 4)), dma((STRIP,)),
                dma((4,)), dma((NSEC,)),
                dma((4,)), dma((NSEC,)),
                dma((NSEC, 4)), dma((NSEC, 4)),
                dma((NSEC,)), dma((NSEC,)),
                dma((STRIP, 3)), dma((STRIP, 3)),
                dma((3, 2)), dma((3, 2)),
                dma((4,)),
            ],
            compiler_params=pltpu.CompilerParams(
                collective_id=0, has_side_effects=True, vmem_limit_bytes=61 << 20
            ),
        )(latent_clips, augment_noise, section_weights, frame_mixing, step_embed)

    return jax.shard_map(
        per_device,
        mesh=mesh,
        in_specs=(
            P("segment", None, "tile", None, None),
            P("segment", None, None, "tile", None, None),
            P("segment", None, None),
            P(),
            P(),
        ),
        out_specs=P("segment", None, "tile", None, None),
        check_vma=False,
    )


def solution(mesh):
    return build(mesh, 8)
```

time: 53.3 us -> 45.8 us (0.86)
  Pallas kernels: 47.9 us -> 44.1 us
  local copies, waits for them, and re-layouts: 5.21 us -> 1.67 us
    pallas_call x1, Pallas kernels: 47.9 us -> 44.1 us  [per_device(): pl.pallas_call(functools.partial(kernel, tiles, per_z), out_shape=jax.Sha...]
    unnamed x11 -> x1, local copies, waits for them, and re-layouts: 5.21 us -> 1.67 us
where the time goes in v1:
time: 45.8 us; the launch traced here: 45.7 us
  Pallas kernels  44.1 us (96%)
  local copies, waits for them, and re-layouts  1.67 us (4%)
    pallas_call x1, Pallas kernels, per_device(): pl.pallas_call(functools.partial(kernel, tiles, per_z), out_shape=jax.Sha...  44.1 us
    unnamed x1, local copies, waits for them, and re-layouts  1.67 us

profile of v1, /device:TPU:2, one launch (start us, length us, event | category | flops | bytes accessed | tf_op | source)
XLA Modules:
  0.0 45.7 jit_solution(9322027651723731184)
XLA Ops:
  0.0 44.1 %shard_map.55 = bf16[1,2,4,128,128]{4,3,2,1,0:T(8,128)(2,1)} custom-call(bf16[1,2,4,128,128]{4,3,2,1,0:T(8,128)(2,1)} %latent_hbm.1, bf16[1,4,2,4,128,128]{5,4,3,2,1,0:T(8,128)(2,1)} %noise_ref.1, bf16[1,1152,128]{2,1,0:T(8,128)(2,1)} %weight_ref.1, f32[6,128]{1,0:T(8,128)} %mix_hbm.1, f32[6,128]{1,0:T(8,128)} %emb_hbm.1), custom_call_target="tpu_custom_call" | custom-call | tf_op jit(solution)/shard_map/pallas_call | solution.py:386
  44.1 1.7 %copy.7 = bf16[1,2,4,128,128]{4,3,2,1,0:T(8,128)(2,1)} copy(bf16[1,2,4,128,128]{4,3,2,1,0:T(8,128)(2,1)} %shard_map.55) | data formatting | bytes 524288

commit v2 on v1

--- a/solution.py
+++ b/solution.py
@@ -12,25 +12,24 @@
 COLS = 128
 FRAMES = 2
 STRIP = 4
-HALO = 6
+HALO = 3
 WIN = STRIP + 2 * HALO
 NSEC = 4
 NSTEP = 6
 SECTION = (0, 0, 0, 1, 2, 3)
-NEDGE = 3
+NEDGE = 2
 NROWS = STRIP + 2 * NEDGE
 SLICE = 9 * C // 8
-GROUPS = {6: (3, 3), 5: (3, 2), 4: (4,), 3: (3,), 2: (2,)}
-WIDEST = 4
-ROW_ORDER = (0, 3, 1, 2)
+SHIFTS = 12
+ROW_ORDER = (1, 2, 0, 3)
 
 norm_eps = 1e-06
 
 
 def kernel(tiles, per_z, latent_hbm, noise_ref, weight_ref, mix_hbm, emb_hbm, out_ref,
-           aug, lat, mxa, mxb, nz, wts, latent_ref, mix_ref, emb_ref, shift,
+           entry, lat, mxa, mxb, nz, wts, latent_ref, mix_ref, emb_ref, shift,
            f_send, f_recv, x_send, x_recv, wx_send, wx_recv, wz_send, wz_recv, wc_send, wc_recv,
-           a_send, a_recv, n_send, n_recv, own_sem):
+           a_send, a_recv, b_send, b_recv, n_send, n_recv, own_sem):
     me = lax.axis_index("segment")
     t = lax.axis_index("tile")
     core = lax.rem(t, 2)
@@ -64,7 +63,7 @@
     barrier = pltpu.get_barrier_semaphore()
     others = [(seg_at(d), t) for d in (1, 2, 3)]
     others += [(me, quad_at(d)) for d in (1, 2, 3)]
-    others += [(me, tile_at(d)) for d in (-2, -1, 1, 2)]
+    others += [(me, tile_at(d)) for d in (-1, 1)]
     for dev in others:
         pl.semaphore_signal(barrier, inc=1, device_id=dev, device_id_type=MESH)
 
@@ -96,7 +95,7 @@
 
     own_weight.start()
     for side in (0, COLS + 8):
-        shift[:, pl.ds(side, 8)] = jnp.zeros((4 * WIDEST, 8, C), jnp.float32)
+        shift[:, pl.ds(side, 8)] = jnp.zeros((SHIFTS, 8, C), jnp.float32)
     pl.semaphore_wait(barrier, len(others))
 
     rows_of = pl.ds(pl.multiple_of(part * SLICE, 16), SLICE)
@@ -131,7 +130,7 @@
             for d in (2, 1, 3):
                 first_to(row, d).start()
 
-    for sec, early in ((1, (3, 1)), (2, (2, 1, 3)), (3, (1, 3))):
+    for sec, early in ((1, (3, 2, 1)), (2, (2, 1, 3)), (3, (1, 3, 2))):
         @pl.when(me == sec)
         def _(early=early):
             for d in early:
@@ -156,33 +155,35 @@
         def _():
             share(sec).wait_recv()
 
-    start_gather(0)
+    for sec in range(NSEC):
+        start_gather(sec)
 
     def row_copy(row, i):
-        far = (14 + row, -2) if row < 2 else (row - 2, 2)
-        to, d = ((10 + row, -1), (2 + row, 1), far)[i]
-        return remote(aug.at[pl.ds(HALO + row, 1)], aug.at[pl.ds(to, 1)],
+        to, d = ((HALO + STRIP + row, -1), (row - 1, 1))[i]
+        return remote(entry.at[0, pl.ds(HALO + row, 1)], entry.at[0, pl.ds(to, 1)],
                       a_send.at[row, i], a_recv.at[row, i], me, tile_at(d))
+
+    def goes(row):
+        return [i for i in range(2) if 0 <= row - i < HALO]
+
+    def strip_copy(i):
+        lo, to, d = ((HALO, HALO + STRIP, -1), (HALO + 1, 0, 1))[i]
+        return remote(entry.at[1, pl.ds(lo, HALO)], entry.at[1, pl.ds(to, HALO)],
+                      b_send.at[i], b_recv.at[i], me, tile_at(d))
 
     for c in own_rest:
         c.wait()
     for row in ROW_ORDER:
         arrived(first_noise(row), f_recv.at[row])
         for f in range(FRAMES):
-            aug[HALO + row, f] = (
+            entry[0, HALO + row, f] = (
                 latent_ref[f, row].astype(jnp.float32)
                 + 0.5 * nz[0, f, NEDGE + row].astype(jnp.float32)
             ).astype(jnp.bfloat16)
-        for i in range(3):
+        for i in goes(row):
             row_copy(row, i).start()
 
-    @pl.when(lax.rem(me, 2) == 1)
-    def _():
-        later_to(2).start()
-
     start_share(0)
-
-    first = t * STRIP - HALO
 
     def put_mixed(dst, row, k, pair, slot):
         change = (0.5 * mix_ref[k:k + 1, :]) * (pair[1] - pair[0])
@@ -194,32 +195,28 @@
             mx[dst][2, row, f] = wide[pl.ds(9, COLS)].astype(jnp.bfloat16)
 
     def blank_outside(dst):
-        zero = jnp.zeros((3, 1, FRAMES, COLS, C), jnp.bfloat16)
-
-        def blank(row, _):
-            mx[dst][:, pl.ds(row, 1)] = zero
-            return 0
-
-        @pl.when(first < 0)
+        zero = jnp.zeros((3, HALO, FRAMES, COLS, C), jnp.bfloat16)
+
+        @pl.when(t == 0)
         def _():
-            lax.fori_loop(0, -first, blank, 0)
-
-        @pl.when(first + WIN > tiles * STRIP)
+            mx[dst][:, pl.ds(0, HALO)] = zero
+
+        @pl.when(t == tiles - 1)
         def _():
-            lax.fori_loop(tiles * STRIP - first, WIN, blank, 0)
-
-    def mix_rows(lo, count):
-        def body(i, _):
-            for j in range(2):
-                row = lo + 2 * i + j
-                put_mixed(0, row, 0, [aug[row, f].astype(jnp.float32) for f in range(FRAMES)], 2 * j)
-            return 0
-        lax.fori_loop(0, count // 2, body, 0)
+            mx[dst][:, pl.ds(HALO + STRIP, HALO)] = zero
+
+    def mix_rows(k, lo, count):
+        for j in range(count):
+            put_mixed(
+                k % 2, lo + j, k,
+                [entry[k // 3, lo + j, f].astype(jnp.float32) for f in range(FRAMES)], 2 * j,
+            )
 
     def step(k, bases=None):
         sec = SECTION[k]
         src, dst = k % 2, (k + 1) % 2
-        lat_in = aug if k == 0 else lat
+        lat_in = entry.at[k // 3] if k % 3 == 0 else lat
+        lat_out = entry.at[1] if k == 2 else lat
         entering = k + 1 < NSTEP and SECTION[k + 1] != sec
 
         def conv_of(base):
@@ -260,7 +257,7 @@
                         for f, v in enumerate(pair)
                     ]
                 for f in range(FRAMES):
-                    lat[row, f] = pair[f]
+                    lat_out[row, f] = pair[f]
                 put_mixed(dst, row, k + 1, [v.astype(jnp.float32) for v in pair], slot + 2 * j)
 
         def several(bases):
@@ -268,89 +265,81 @@
             for i, base in enumerate(bases):
                 finish(base, accs[i], 4 * i)
 
-        def run(lo, groups):
-            times = len(groups) if len(set(groups)) == 1 else 1
-            if times == 1:
-                for take in groups:
-                    several([lo + 2 * i for i in range(take)])
-                    lo += 2 * take
-                return
-            take = groups[0]
-
-            def body(p, _):
-                several([lo + 2 * (p * take + i) for i in range(take)])
-                return 0
-
-            lax.fori_loop(0, times, body, 0)
-
-        if bases is not None:
+        if bases is None:
+            several([k % 3 + 2 * i for i in range(4 - k % 3)])
+        else:
             several(bases)
-        else:
-            run(k, GROUPS[(WIN - 2 * (k + 1)) // 2])
-        if k < NSTEP - 1 and bases is None:
-            blank_outside(dst)
-
-    edge = {}
+
+    def edge_copy(sec, i):
+        count = NSEC - sec
+        lo, to, d = (
+            (NEDGE, NEDGE + STRIP, -1),
+            (NEDGE + STRIP - count, NEDGE - count, 1),
+        )[i]
+        return remote(nz.at[sec, :, pl.ds(lo, count)], nz.at[sec, :, pl.ds(to, count)],
+                      n_send.at[sec, i], n_recv.at[sec, i], me, tile_at(d))
 
     def forward_noise(sec):
-        count = NEDGE - (sec - 1)
         arrived(later_noise(sec), x_recv.at[sec])
-        for i, (lo, to, d) in enumerate(
-            ((NEDGE, NEDGE + STRIP, -1), (NEDGE + STRIP - count, NEDGE - count, 1))
-        ):
-            edge[sec, i] = remote(
-                nz.at[sec, :, pl.ds(lo, count)], nz.at[sec, :, pl.ds(to, count)],
-                n_send.at[sec - 1, i], n_recv.at[sec - 1, i], me, tile_at(d),
-            )
-            edge[sec, i].start()
+        for i in range(2):
+            edge_copy(sec, i).start()
 
     def wait_edge(sec):
         for i in range(2):
-            edge[sec, i].wait_recv()
-
-    chip = HALO - STRIP * core
-    mix_rows(HALO, STRIP)
-    near = (HALO + STRIP) - 2 * STRIP * core
-    for row in range(STRIP):
-        arrived(aug.at[pl.ds(near + row, 1)], a_recv.at[row, core])
-    mix_rows(near, STRIP)
+            edge_copy(sec, i).wait_recv()
+
+    near = (HALO + STRIP) * (1 - core)
+    over = (HALO + STRIP) * core
+    inner = (1 - core) * STRIP
+    outer = core * STRIP
+
+    mix_rows(0, HALO, STRIP)
+    for row in range(HALO):
+        arrived(entry.at[0, pl.ds(near + row, 1)], a_recv.at[row + core, core])
+    mix_rows(0, near, HALO)
     own_weight.wait()
     finish_share(0)
-    step(0, [chip + 2 * i for i in range(3)])
-    for sec in (1, 2, 3):
-        start_gather(sec)
-    over = (HALO - STRIP) + 2 * STRIP * core
-    for row in range(STRIP):
-        arrived(aug.at[pl.ds(over + row, 1)], a_recv.at[row, 1 - core])
-    mix_rows(over, STRIP)
-    for row in range(STRIP):
-        row_copy(row, 2).wait_recv()
-    mix_rows(0, 2)
-    mix_rows(WIN - 2, 2)
+    step(0, [inner, inner + 2])
+    for row in range(HALO):
+        arrived(entry.at[0, pl.ds(over + row, 1)], a_recv.at[row + 1 - core, 1 - core])
+    mix_rows(0, over, HALO)
     blank_outside(0)
-    step(0, [lax.rem(chip + 6 + 2 * i, 14) for i in range(4)])
+    step(0, [outer, outer + 2])
     blank_outside(1)
-    forward_noise(1)
+    forward_noise(2)
+    forward_noise(3)
     step(1)
+    blank_outside(0)
+    arrived(later_noise(1), x_recv.at[1])
+    step(2)
+    for i in range(2):
+        strip_copy(i).start()
+
     for sec in (1, 2, 3):
         start_share(sec)
-    forward_noise(2)
-    forward_noise(3)
-    wait_edge(1)
-    step(2)
+    arrived(entry.at[1, pl.ds(near, HALO)], b_recv.at[core])
+    mix_rows(3, near, HALO)
     finish_share(1)
     wait_edge(2)
-    step(3)
+    step(3, [inner, inner + 2])
+    arrived(entry.at[1, pl.ds(over, HALO)], b_recv.at[1 - core])
+    mix_rows(3, over, HALO)
+    blank_outside(1)
+    step(3, [outer, outer + 2])
+    blank_outside(0)
     finish_share(2)
     wait_edge(3)
     step(4)
+    blank_outside(1)
     finish_share(3)
     step(5)
 
     for d in (1, 2, 3):
         slice_to(d).wait_send()
-        for i in range(2):
-            edge[d, i].wait_send()
+    for i in range(2):
+        strip_copy(i).wait_send()
+        for sec in (2, 3):
+            edge_copy(sec, i).wait_send()
 
     @pl.when(me == 0)
     def _():
@@ -371,7 +360,7 @@
             share(sec).wait_send()
 
     for row in range(STRIP):
-        for i in range(3):
+        for i in goes(row):
             row_copy(row, i).wait_send()
 
 
@@ -389,7 +378,7 @@
             in_specs=[hbm, hbm, hbm, hbm, hbm],
             out_specs=vmem,
             scratch_shapes=[
-                pltpu.VMEM((WIN, FRAMES, COLS, C), bf),
+                pltpu.VMEM((2, WIN, FRAMES, COLS, C), bf),
                 pltpu.VMEM((WIN, FRAMES, COLS, C), bf),
                 pltpu.VMEM((3, WIN, FRAMES, COLS, C), bf),
                 pltpu.VMEM((3, WIN, FRAMES, COLS, C), bf),
@@ -398,14 +387,15 @@
                 pltpu.VMEM((FRAMES, STRIP, COLS, C), bf),
                 pltpu.VMEM((NSTEP, C), jnp.float32),
                 pltpu.VMEM((NSTEP, C), jnp.float32),
-                pltpu.VMEM((4 * WIDEST, COLS + 16, C), jnp.float32),
+                pltpu.VMEM((SHIFTS, COLS + 16, C), jnp.float32),
                 dma((STRIP, 4)), dma((STRIP,)),
                 dma((4,)), dma((NSEC,)),
                 dma((4,)), dma((NSEC,)),
                 dma((NSEC, 4)), dma((NSEC, 4)),
                 dma((NSEC,)), dma((NSEC,)),
-                dma((STRIP, 3)), dma((STRIP, 3)),
-                dma((3, 2)), dma((3, 2)),
+                dma((STRIP, 2)), dma((STRIP, 2)),
+                dma((2,)), dma((2,)),
+                dma((NSEC, 2)), dma((NSEC, 2)),
                 dma((4,)),
             ],
             compiler_params=pltpu.CompilerParams(

time: 45.8 us -> 41.2 us (0.90)
  Pallas kernels: 44.1 us -> 39.4 us
    pallas_call x1, Pallas kernels: 44.1 us -> 39.4 us  [per_device(): pl.pallas_call(functools.partial(kernel, tiles, per_z), out_shape=jax.Sha...]
where the time goes in v2:
time: 41.2 us; the launch traced here: 41.1 us
  Pallas kernels  39.4 us (96%)
  local copies, waits for them, and re-layouts  1.67 us (4%)
    pallas_call x1, Pallas kernels, per_device(): pl.pallas_call(functools.partial(kernel, tiles, per_z), out_shape=jax.Sha...  39.4 us
    unnamed x1, local copies, waits for them, and re-layouts  1.67 us

profile of v2, /device:TPU:2, one launch (start us, length us, event | category | flops | bytes accessed | tf_op | source)
XLA Modules:
  0.0 41.1 jit_solution(15364237301856556387)
XLA Ops:
  0.0 39.4 %shard_map.55 = bf16[1,2,4,128,128]{4,3,2,1,0:T(8,128)(2,1)} custom-call(bf16[1,2,4,128,128]{4,3,2,1,0:T(8,128)(2,1)} %latent_hbm.1, bf16[1,4,2,4,128,128]{5,4,3,2,1,0:T(8,128)(2,1)} %noise_ref.1, bf16[1,1152,128]{2,1,0:T(8,128)(2,1)} %weight_ref.1, f32[6,128]{1,0:T(8,128)} %mix_hbm.1, f32[6,128]{1,0:T(8,128)} %emb_hbm.1), custom_call_target="tpu_custom_call" | custom-call | tf_op jit(solution)/shard_map/pallas_call | solution.py:375
  39.4 1.7 %copy.7 = bf16[1,2,4,128,128]{4,3,2,1,0:T(8,128)(2,1)} copy(bf16[1,2,4,128,128]{4,3,2,1,0:T(8,128)(2,1)} %shard_map.55) | data formatting | bytes 524288

commit v3 on v2

--- a/solution.py
+++ b/solution.py
@@ -374,7 +374,7 @@
         hbm = pl.BlockSpec(memory_space=pltpu.HBM)
         return pl.pallas_call(
             functools.partial(kernel, tiles, per_z),
-            out_shape=jax.ShapeDtypeStruct(latent_clips.shape, bf),
+            out_shape=pltpu.VMEM(latent_clips.shape, bf),
             in_specs=[hbm, hbm, hbm, hbm, hbm],
             out_specs=vmem,
             scratch_shapes=[

time: 41.2 us -> 39.5 us (0.959)
  local copies, waits for them, and re-layouts: 1.67 us -> 0.71 us
  Pallas kernels: 39.4 us -> 38.8 us
    unnamed x1, local copies, waits for them, and re-layouts: 1.67 us -> 0.71 us
    pallas_call x1, Pallas kernels: 39.4 us -> 38.8 us  [per_device(): pl.pallas_call(functools.partial(kernel, tiles, per_z), out_shape=pltpu.V...]
where the time goes in v3:
time: 39.5 us
  Pallas kernels  38.8 us (98%)
  local copies, waits for them, and re-layouts  0.71 us (2%)
    pallas_call x1, Pallas kernels, per_device(): pl.pallas_call(functools.partial(kernel, tiles, per_z), out_shape=pltpu.V...  38.8 us

profile of v3, /device:TPU:2, one launch (start us, length us, event | category | flops | bytes accessed | tf_op | source)
XLA Modules:
  0.0 39.5 jit_solution(3202349680295590958)
XLA Ops:
  0.0 38.8 %shard_map.55 = bf16[1,2,4,128,128]{4,3,2,1,0:T(8,128)(2,1)S(1)} custom-call(bf16[1,2,4,128,128]{4,3,2,1,0:T(8,128)(2,1)} %latent_hbm.1, bf16[1,4,2,4,128,128]{5,4,3,2,1,0:T(8,128)(2,1)} %noise_ref.1, bf16[1,1152,128]{2,1,0:T(8,128)(2,1)} %weight_ref.1, f32[6,128]{1,0:T(8,128)} %mix_hbm.1, f32[6,128]{1,0:T(8,128)} %emb_hbm.1), custom_call_target="tpu_custom_call" | custom-call | tf_op jit(solution)/shard_map/pallas_call | solution.py:375
  38.8 0.7 %copy.7 = bf16[1,2,4,128,128]{4,3,2,1,0:T(8,128)(2,1)} copy(bf16[1,2,4,128,128]{4,3,2,1,0:T(8,128)(2,1)S(1)} %shard_map.55) | data formatting | bytes 524288

commit v4 on v3

--- a/solution.py
+++ b/solution.py
@@ -167,9 +167,12 @@
         return [i for i in range(2) if 0 <= row - i < HALO]
 
     def strip_copy(i):
-        lo, to, d = ((HALO, HALO + STRIP, -1), (HALO + 1, 0, 1))[i]
-        return remote(entry.at[1, pl.ds(lo, HALO)], entry.at[1, pl.ds(to, HALO)],
-                      b_send.at[i], b_recv.at[i], me, tile_at(d))
+        lo = (HALO + 2 * core, HALO + 2 - core, HALO + 1 - core)[i]
+        count = (2, 1, HALO)[i]
+        away = STRIP - 2 * STRIP * core
+        to, device = (lo + away, tile_at(2 * core - 1)) if i < 2 else (lo - away, partner)
+        return remote(entry.at[1, pl.ds(lo, count)], entry.at[1, pl.ds(to, count)],
+                      b_send.at[i], b_recv.at[i], me, device)
 
     for c in own_rest:
         c.wait()
@@ -311,21 +314,27 @@
     step(1)
     blank_outside(0)
     arrived(later_noise(1), x_recv.at[1])
-    step(2)
-    for i in range(2):
-        strip_copy(i).start()
+    step(2, [2 + 2 * core])
+    strip_copy(0).start()
+    step(2, [4 - 2 * core])
+    strip_copy(1).start()
+    strip_copy(2).start()
 
     for sec in (1, 2, 3):
         start_share(sec)
-    arrived(entry.at[1, pl.ds(near, HALO)], b_recv.at[core])
+    arrived(entry.at[1, pl.ds(near, HALO)], b_recv.at[2])
     mix_rows(3, near, HALO)
     finish_share(1)
     wait_edge(2)
     step(3, [inner, inner + 2])
-    arrived(entry.at[1, pl.ds(over, HALO)], b_recv.at[1 - core])
-    mix_rows(3, over, HALO)
+    arrived(entry.at[1, pl.ds(over + 1 - core, 2)], b_recv.at[0])
+    mix_rows(3, over + 1 - core, 2)
     blank_outside(1)
-    step(3, [outer, outer + 2])
+    step(3, [outer + 2 - 2 * core])
+    arrived(entry.at[1, pl.ds(over + 2 * core, 1)], b_recv.at[1])
+    mix_rows(3, over + 2 * core, 1)
+    blank_outside(1)
+    step(3, [outer + 2 * core])
     blank_outside(0)
     finish_share(2)
     wait_edge(3)
@@ -336,8 +345,9 @@
 
     for d in (1, 2, 3):
         slice_to(d).wait_send()
+    for i in range(3):
+        strip_copy(i).wait_send()
     for i in range(2):
-        strip_copy(i).wait_send()
         for sec in (2, 3):
             edge_copy(sec, i).wait_send()
 
@@ -394,7 +404,7 @@
                 dma((NSEC, 4)), dma((NSEC, 4)),
                 dma((NSEC,)), dma((NSEC,)),
                 dma((STRIP, 2)), dma((STRIP, 2)),
-                dma((2,)), dma((2,)),
+                dma((3,)), dma((3,)),
                 dma((NSEC, 2)), dma((NSEC, 2)),
                 dma((4,)),
             ],

time: 39.5 us -> 39.2 us (level)
  Pallas kernels: 38.8 us -> 38.4 us
where the time goes in v4:
time: 39.2 us
  Pallas kernels  38.4 us (98%)
  local copies, waits for them, and re-layouts  0.71 us (2%)
    pallas_call x1, Pallas kernels, per_device(): pl.pallas_call(functools.partial(kernel, tiles, per_z), out_shape=pltpu.V...  38.4 us

profile of v4, /device:TPU:2, one launch (start us, length us, event | category | flops | bytes accessed | tf_op | source)
XLA Modules:
  0.0 39.2 jit_solution(7676962175869249071)
XLA Ops:
  0.0 38.4 %shard_map.55 = bf16[1,2,4,128,128]{4,3,2,1,0:T(8,128)(2,1)S(1)} custom-call(bf16[1,2,4,128,128]{4,3,2,1,0:T(8,128)(2,1)} %latent_hbm.1, bf16[1,4,2,4,128,128]{5,4,3,2,1,0:T(8,128)(2,1)} %noise_ref.1, bf16[1,1152,128]{2,1,0:T(8,128)(2,1)} %weight_ref.1, f32[6,128]{1,0:T(8,128)} %mix_hbm.1, f32[6,128]{1,0:T(8,128)} %emb_hbm.1), custom_call_target="tpu_custom_call" | custom-call | tf_op jit(solution)/shard_map/pallas_call | solution.py:385
  38.5 0.7 %copy.7 = bf16[1,2,4,128,128]{4,3,2,1,0:T(8,128)(2,1)} copy(bf16[1,2,4,128,128]{4,3,2,1,0:T(8,128)(2,1)S(1)} %shard_map.55) | data formatting | bytes 524288

commit v5 on v4

--- a/solution.py
+++ b/solution.py
@@ -130,7 +130,7 @@
             for d in (2, 1, 3):
                 first_to(row, d).start()
 
-    for sec, early in ((1, (3, 2, 1)), (2, (2, 1, 3)), (3, (1, 3, 2))):
+    for sec, early in ((1, (3, 1)), (2, (2, 1, 3)), (3, (1, 3))):
         @pl.when(me == sec)
         def _(early=early):
             for d in early:
@@ -185,6 +185,10 @@
             ).astype(jnp.bfloat16)
         for i in goes(row):
             row_copy(row, i).start()
+
+    @pl.when(lax.rem(me, 2) == 1)
+    def _():
+        later_to(2).start()
 
     start_share(0)
 
@@ -310,7 +314,6 @@
     step(0, [outer, outer + 2])
     blank_outside(1)
     forward_noise(2)
-    forward_noise(3)
     step(1)
     blank_outside(0)
     arrived(later_noise(1), x_recv.at[1])
@@ -319,6 +322,7 @@
     step(2, [4 - 2 * core])
     strip_copy(1).start()
     strip_copy(2).start()
+    forward_noise(3)
 
     for sec in (1, 2, 3):
         start_share(sec)

time: 39.2 us -> 39.7 us (1.013); the launches traced: 39.2 us -> 39.1 us
  no operation moved by 1% of the time
where the time goes in v5:
time: 39.7 us; the launch traced here: 39.1 us
  Pallas kernels  38.4 us (97%)
  local copies, waits for them, and re-layouts  0.71 us (2%)
    pallas_call x1, Pallas kernels, per_device(): pl.pallas_call(functools.partial(kernel, tiles, per_z), out_shape=pltpu.V...  38.4 us

profile of v5, /device:TPU:2, one launch (start us, length us, event | category | flops | bytes accessed | tf_op | source)
XLA Modules:
  0.0 39.1 jit_solution(5005177877224967524)
XLA Ops:
  0.0 38.4 %shard_map.55 = bf16[1,2,4,128,128]{4,3,2,1,0:T(8,128)(2,1)S(1)} custom-call(bf16[1,2,4,128,128]{4,3,2,1,0:T(8,128)(2,1)} %latent_hbm.1, bf16[1,4,2,4,128,128]{5,4,3,2,1,0:T(8,128)(2,1)} %noise_ref.1, bf16[1,1152,128]{2,1,0:T(8,128)(2,1)} %weight_ref.1, f32[6,128]{1,0:T(8,128)} %mix_hbm.1, f32[6,128]{1,0:T(8,128)} %emb_hbm.1), custom_call_target="tpu_custom_call" | custom-call | tf_op jit(solution)/shard_map/pallas_call | solution.py:389
  38.4 0.7 %copy.7 = bf16[1,2,4,128,128]{4,3,2,1,0:T(8,128)(2,1)} copy(bf16[1,2,4,128,128]{4,3,2,1,0:T(8,128)(2,1)S(1)} %shard_map.55) | data formatting | bytes 524288
